TPU v7x, 256 devices: a whole 4x4x8 slice. The times are simulated.
256 devices in a mesh: row: 8 (over z), col: 32 (over y, x, core).
Axes of the slice: x: 4, y: 4, z: 8, core: 2. Of those that a mesh axis runs over, the one named last changes fastest.
Arguments:
- flow_state: float32 [125, 5, 32768], P(None, None, ('row', 'col'))
- cot_final: float32 [125, 5, 32768], P(None, None, ('row', 'col')), may hold values from -6 to 6
- metric: float32 [32768], P(('row', 'col')), may hold values from 1 to 4
- send_col: int32 [256, 160], P(('row', 'col')), may hold values from 0 to 768, as said below
- send_row: int32 [256, 64], P(('row', 'col')), may hold values from 0 to 768, as said below
- exterior: int32 [256, 768], P(('row', 'col')), may hold values from 0 to 991, as said below
- face_kind: int32 [256, 768], P(('row', 'col')), may hold values from 0 to 3, as said below
- mortar_fine: int32 [256, 128], P(('row', 'col')), may hold values from 0 to 768, as said below
- mortar_coarse: int32 [256, 32], P(('row', 'col')), may hold values from 0 to 768, as said below
Outputs:
- cot_state: float32 [125, 5, 32768], P(None, None, ('row', 'col'))
Inputs may be any that keep to these rules, and one draw needn't show every extreme that they name: `send_col`: each device lists, for each col peer h in order, 5 slots: slots 0 to 1 hold its +x faces whose partner is a -x face of h, the next 2 its -x faces whose partner is a +x face of h, the last 1 its +z faces that are coarse sides of mortars whose fine faces lie on h (slot 4 + i is mortar i of the pair); partners are listed in the same order on both sides; unused slots hold 768; some pair of devices fills every slot. `send_row`: likewise for row peers: slots 0 to 3 hold +y faces paired with -y faces of the peer, the next 4 -y faces paired with +y faces; unused slots hold 768. `exterior`: for a conforming face, the position of its partner's trace in the device's table; partners are symmetric and have opposite normals; wall and mortar faces name themselves. `face_kind`: 0 conforming, 1 wall, 2 fine side of a mortar (a -z face), 3 coarse side of a mortar (a +z face). `mortar_fine`: entry q * 32 + h + i is the fine face of quadrant q of mortar i whose coarse face lies on col peer h; mortars of a pair are numbered from 0; unused entries hold 768; every fine face appears at most once. `mortar_coarse`: entry h + i is the coarse face of mortar i whose fine faces lie on col peer h; unused entries hold 768.
All inputs are finite; a program needn't handle non-finite values.
Results may differ from a plain program's by a relative error of at most 0.0003.
Values sent between devices are 32-bit elements; how exact they have to be, the bound alone decides.
A program may use at most 128 MiB of HBM per device.

v0:
```python
import functools
import math

import jax
import jax.numpy as jnp
import numpy as np
from jax import lax
from jax.experimental import pallas as pl
from jax.experimental.pallas import tpu as pltpu
from jax.sharding import PartitionSpec as P

STEP = 0.005
W_END = 0.1
COL_ROWS = 16
ROW_ROWS = 8
LANES = 128
GROUPS = 7
WIDE = GROUPS * LANES
MESH = pl.DeviceIdType.MESH
F32 = jnp.float32
BF16 = jnp.bfloat16
FIELD_ORDER = ((0, 1, 2, 3, 4), (0, 2, 1, 3, 4), (0, 3, 1, 2, 4))


def basis():
    inner = math.sqrt(3.0 / 7.0)
    x = np.array([-1.0, -inner, 0.0, inner, 1.0])
    w = np.array([0.1, 49.0 / 90.0, 32.0 / 45.0, 49.0 / 90.0, 0.1])

    def lagrange(at):
        out = np.ones((5, 5))
        for m in range(5):
            for n in range(5):
                if n != m:
                    out[:, m] *= (at - x[n]) / (x[m] - x[n])
        return out

    eye = np.eye(5)
    gaps = x[:, None] - x[None, :] + eye
    bary = 1.0 / np.prod(gaps, axis=1)
    diff = bary[None, :] / bary[:, None] / gaps * (1.0 - eye)
    diff = diff - eye * diff.sum(axis=1)[:, None]
    halves = [lagrange((x + 2.0 * a - 1.0) / 2.0) for a in (0, 1)]
    projs = [0.5 * (m.T * w[None, :]) / w[:, None] for m in halves]
    interp = [np.kron(halves[a], halves[b]) for a in (0, 1) for b in (0, 1)]
    project = [np.kron(projs[a], projs[b]) for a in (0, 1) for b in (0, 1)]
    return diff, interp, project


def stencil_tables():
    diff = basis()[0]
    parts = []
    for matrix in (diff, diff.T):
        along = np.zeros((5, 8))
        along[:, :5] = matrix.T
        parts.append(along.reshape(40))
        parts.append(np.repeat(matrix.reshape(25), 8))
    column = np.concatenate(parts)
    return np.repeat(column[:, None], LANES, axis=1).astype(np.float32)


def mortar_tables():
    _, interp, project = basis()
    out = np.zeros((4, 4, LANES, LANES))
    for q in range(4):
        for at, matrix in enumerate(
            (interp[q], project[q].T, project[q], interp[q].T)
        ):
            out[at, q, :125, :125] = np.kron(np.eye(5), matrix)
    out = out.reshape(4, 4 * LANES, LANES).astype(np.float32)
    high = out.astype(jnp.bfloat16)
    low = (out - high.astype(np.float32)).astype(jnp.bfloat16)
    return high, low


def split(x):
    high = x.astype(BF16)
    return high, (x - high.astype(F32)).astype(BF16)


def split_rows(x):
    return jnp.concatenate(split(x), axis=0)


def dot(a, b):
    return lax.dot_general(a, b, (((1,), (0,)), ((), ())), preferred_element_type=F32)


def dot_nt(a, b):
    return lax.dot_general(a, b, (((1,), (1,)), ((), ())), preferred_element_type=F32)


def pick(x, onehot):
    both = dot(split_rows(x), onehot)
    return both[: x.shape[0]] + both[x.shape[0] :]


def place(x, onehot):
    both = dot_nt(split_rows(x), onehot)
    return both[: x.shape[0]] + both[x.shape[0] :]


def rows_at(start, size=8):
    return pl.ds(pl.multiple_of(start, 8), size)


def kernel(
    nr, nc, send_width,
    u_ref, c_ref, met_ref, int_ref, tab_ref, khi_ref, klo_ref,
    out_ref,
    u1_ref, acc_ref, fz_ref, own_ref, ext_ref, val_ref, tc_ref, xc_ref, vc_ref,
    ohs_ref, ohr_ref, ohl_ref, lane_ref,
    sbuf, rbuf, send_sem, recv_sem,
):
    mr = lax.axis_index("row")
    mc = lax.axis_index("col")
    barrier = pltpu.get_barrier_semaphore()

    def greet_col(k, carry):
        pl.semaphore_signal(
            barrier, inc=1, device_id=(mr, lax.rem(mc + k, nc)), device_id_type=MESH
        )
        return carry

    def greet_row(k, carry):
        pl.semaphore_signal(
            barrier, inc=1, device_id=(lax.rem(mr + k, nr), mc), device_id_type=MESH
        )
        return carry

    lax.fori_loop(1, nc, greet_col, 0)
    lax.fori_loop(1, nr, greet_row, 0)

    chunks = send_width // LANES
    at_ext = chunks
    at_sel = at_ext + 6
    at_kind = at_sel + 2
    at_fine = at_kind + 6
    at_coarse = at_fine + 1
    moved_rows = COL_ROWS * (nc - 1) + ROW_ROWS * (nr - 1)

    def onehot(target, rows, base=0):
        iota = lax.broadcasted_iota(jnp.int32, (rows, LANES), 0) + base
        return jnp.where(iota == target, 1.0, 0.0).astype(BF16)

    for n in range(chunks):
        ohs_ref[:, n * LANES : (n + 1) * LANES] = onehot(int_ref[n : n + 1, :], 768)
    for k in range(6):
        target = int_ref[at_ext + k : at_ext + k + 1, :]
        ohl_ref[k] = onehot(target, LANES)
        remote = target if k < 4 else int_ref[at_sel + k - 4 : at_sel + k - 3, :] + LANES
        ohr_ref[:, k * LANES : (k + 1) * LANES] = onehot(remote, send_width, LANES)
    fine_list = int_ref[at_fine : at_fine + 1, :]
    coarse_list = int_ref[at_coarse : at_coarse + 1, :]
    ohl_ref[6] = onehot(fine_list - 512, LANES)
    ohl_ref[7] = onehot(coarse_list - 640, LANES)

    for k in range(GROUPS):
        lanes = slice(k * LANES, (k + 1) * LANES)
        one = jnp.ones((1, LANES), F32)
        if k < 6:
            kind = int_ref[at_kind + k : at_kind + k + 1, :]
            rows = [
                one * (2.0 * (k % 2) - 1.0),
                jnp.where(kind == 3, -1.0, 1.0),
                one,
                jnp.where((kind == 0) | (kind == 2), 1.0, 0.0),
                jnp.where(kind == 1, 1.0, 0.0),
                one,
                met_ref[...] * (1.0 / W_END),
            ]
        else:
            valid = jnp.where(coarse_list < 768, 1.0, 0.0)
            rows = [one, -one, -one, one, 0.0 * one, valid, one]
        for n, row in enumerate(rows):
            lane_ref[n : n + 1, lanes] = row

    for e in range(4):
        tc_ref[e, 120:128, :] = jnp.zeros((8, 768), F32)
        rbuf[e, nc * COL_ROWS + nr * ROW_ROWS :, :] = jnp.zeros(
            (send_width - nc * COL_ROWS - nr * ROW_ROWS, LANES), F32
        )
    vc_ref[120:128, :] = jnp.zeros((8, LANES), F32)


    def post(e, src_ref, scale):
        def take(a, carry):
            for k in range(6):
                d, h = k // 2, k % 2
                lanes = slice(k * LANES, (k + 1) * LANES)
                for f in range(5):
                    base = 200 * FIELD_ORDER[d][f]
                    if d == 0:
                        piece = src_ref[pl.ds(base + 40 * a + 4 * h, 5, 8), :]
                    elif d == 1:
                        piece = src_ref[rows_at(base + 40 * a + 32 * h), :]
                    else:
                        piece = src_ref[rows_at(base + 160 * h + 8 * a), :]
                    if scale is not None:
                        piece = piece * (met_ref[...] * (scale / W_END))
                    own_ref[e, 5 * f + a, : piece.shape[0], lanes] = piece
            return carry

        lax.fori_loop(0, 5, take, 0)
        for g in range(25):
            tc_ref[e, 5 * g : 5 * g + 5, :] = own_ref[e, g, 0:5, 0:768]
        both = split_rows(tc_ref[e])
        sent = dot(both, ohs_ref[...])
        sent = sent[:LANES] + sent[LANES:]
        for n in range(chunks):
            sbuf[e, n * LANES : (n + 1) * LANES, :] = sent[:, n * LANES : (n + 1) * LANES].T
        if e == 0:
            pl.semaphore_wait(barrier, nc + nr - 2)

        def push_col(k, carry):
            peer = lax.rem(mc + k, nc)
            pltpu.make_async_remote_copy(
                src_ref=sbuf.at[e, rows_at(COL_ROWS * peer, COL_ROWS)],
                dst_ref=rbuf.at[e, rows_at(COL_ROWS * mc, COL_ROWS)],
                send_sem=send_sem.at[e],
                recv_sem=recv_sem.at[e],
                device_id=(mr, peer),
                device_id_type=MESH,
            ).start()
            return carry

        def push_row(k, carry):
            peer = lax.rem(mr + k, nr)
            pltpu.make_async_remote_copy(
                src_ref=sbuf.at[e, rows_at(COL_ROWS * nc + ROW_ROWS * peer, ROW_ROWS)],
                dst_ref=rbuf.at[e, rows_at(COL_ROWS * nc + ROW_ROWS * mr, ROW_ROWS)],
                send_sem=send_sem.at[e],
                recv_sem=recv_sem.at[e],
                device_id=(peer, mc),
                device_id_type=MESH,
            ).start()
            return carry

        lax.fori_loop(1, nc, push_col, 0)
        lax.fori_loop(1, nr, push_row, 0)
        own_col = rows_at(COL_ROWS * mc, COL_ROWS)
        rbuf[e, own_col, :] = sbuf[e, own_col, :]
        own_row = rows_at(COL_ROWS * nc + ROW_ROWS * mr, ROW_ROWS)
        rbuf[e, own_row, :] = sbuf[e, own_row, :]
        for k in range(6):
            other = k ^ 1
            got = dot(both[:, other * LANES : (other + 1) * LANES], ohl_ref[k])
            xc_ref[e, :, k * LANES : (k + 1) * LANES] = got[:LANES] + got[LANES:]
        got = dot(both[:, 5 * LANES : 6 * LANES], ohl_ref[7])
        xc_ref[e, :, 7 * LANES :] = got[:LANES] + got[LANES:]

    quarter = lax.broadcasted_iota(jnp.int32, (1, LANES), 1) // nc

    def by_quarter(at, x):
        width = x.shape[1] // LANES
        hi, lo = split(x)
        k_hi, k_lo = khi_ref[at], klo_ref[at]
        full = dot(k_hi, hi) + (dot(k_lo, hi) + dot(k_hi, lo))
        out = []
        for n in range(width):
            total = jnp.zeros((LANES, LANES), F32)
            for q in range(4):
                block = full[q * LANES : (q + 1) * LANES, n * LANES : (n + 1) * LANES]
                total = total + jnp.where(quarter == q, block, 0.0)
            out.append(total)
        return out

    def finish(e, table):
        size = pl.ds(0, moved_rows)
        whole = pltpu.make_async_copy(sbuf.at[e, size], rbuf.at[e, size], recv_sem.at[e])
        whole.wait()
        came = jnp.concatenate(
            [rbuf[e, n * LANES : (n + 1) * LANES, :].T for n in range(chunks)], axis=1
        )
        got = pick(came, ohr_ref[...])
        for k in range(4):
            lanes = slice(k * LANES, (k + 1) * LANES)
            xc_ref[e, :, lanes] = xc_ref[e, :, lanes] + got[:, lanes]
        xc_ref[e, :, 6 * LANES : 7 * LANES] = got[:, 5 * LANES :]
        coarse = jnp.concatenate([got[:, 4 * LANES : 5 * LANES], xc_ref[e, :, 7 * LANES :]], axis=1)
        fine_side, coarse_side = by_quarter(table, coarse)
        lanes = slice(4 * LANES, 5 * LANES)
        xc_ref[e, :, lanes] = xc_ref[e, :, lanes] + place(fine_side, ohl_ref[6])
        xc_ref[e, :, 7 * LANES :] = coarse_side
        for g in range(25):
            ext_ref[e, g] = xc_ref[e, 5 * g : 5 * g + 8, 0:WIDE]
            own_ref[e, g, :, 6 * LANES :] = xc_ref[e, 5 * g : 5 * g + 8, WIDE:]

    def sent_all(e):
        size = pl.ds(0, moved_rows)
        pltpu.make_async_copy(sbuf.at[e, size], rbuf.at[e, size], send_sem.at[e]).wait()


    def lane_row(n):
        return lane_ref[n : n + 1, :]

    def both_states(e, a):
        own = [own_ref[e, 5 * f + a] for f in range(5)]
        ext = [ext_ref[e, 5 * f + a] for f in range(5)]
        return own, ext

    def fill_states(e, a):
        own, ext = both_states(e, a)
        gathered = lane_row(3) > 0.5
        valid = lane_row(5) > 0.5
        flip = 1.0 - 2.0 * lane_row(4)
        default = (1.0, 0.0, 0.0, 0.0, 1.0)
        own = [jnp.where(valid, own[f], default[f]) for f in range(5)]
        mirror = [own[f] * flip if f == 1 else own[f] for f in range(5)]
        ext = [jnp.where(gathered, ext[f], mirror[f]) for f in range(5)]
        ext = [jnp.where(valid, ext[f], default[f]) for f in range(5)]
        return own, ext

    def primitives(s):
        inv = 1.0 / s[0]
        vel = [s[1] * inv, s[2] * inv, s[3] * inv]
        square = vel[0] * vel[0] + vel[1] * vel[1] + vel[2] * vel[2]
        pressure = 0.4 * (s[4] - 0.5 * (s[1] * vel[0] + s[2] * vel[1] + s[3] * vel[2]))
        return inv, vel, square, pressure

    def face_flux(e):
        def body(a, carry):
            own, ext = fill_states(e, a)
            orient, sign = lane_row(0), lane_row(1)
            fluxes, parts = [], []
            for s in (own, ext):
                inv, vel, _, pressure = primitives(s)
                fluxes.append(
                    (
                        s[1],
                        s[1] * vel[0] + pressure,
                        s[2] * vel[0],
                        s[3] * vel[0],
                        (s[4] + pressure) * vel[0],
                    )
                )
                parts.append(vel[0] * vel[0] + 1.4 * pressure * inv)
            speed = jnp.sqrt(0.5 * (parts[0] + parts[1]))
            for f in range(5):
                val_ref[5 * f + a] = 0.5 * (
                    orient * (fluxes[0][f] - sign * fluxes[1][f])
                    + sign * speed * (ext[f] - own[f])
                )
            return carry

        lax.fori_loop(0, 5, body, 0)

    def face_adjoint(state, cot):
        def body(a, carry):
            own, ext = fill_states(state, a)
            y, y_ext = both_states(cot, a)
            gathered = lane_row(3) > 0.5
            flip = 1.0 - 2.0 * lane_row(4)
            y_ext = [
                jnp.where(gathered, y_ext[f], y[f] * flip if f == 1 else y[f]) for f in range(5)
            ]
            orient, sign = lane_row(0), lane_row(2)
            inv, vel, square, pressure = primitives(own)
            inv_b, vel_b, _, pressure_b = primitives(ext)
            sound = 1.4 * pressure * inv
            speed2 = 0.5 * (
                vel[0] * vel[0] + vel_b[0] * vel_b[0] + sound + 1.4 * pressure_b * inv_b
            )
            speed = jnp.sqrt(speed2)
            plus = [orient * (y_ext[f] + sign * y[f]) for f in range(5)]
            minus = [y[f] - y_ext[f] for f in range(5)]
            dots = minus[0] * (ext[0] - own[0])
            for f in range(1, 5):
                dots = dots + minus[f] * (ext[f] - own[f])
            spread = 0.5 * dots * inv / speed
            p_bar = plus[1] + plus[4] * vel[0]
            along = plus[1] * vel[0] + plus[2] * vel[1] + plus[3] * vel[2]
            along = along + plus[4] * (own[4] + pressure) * inv
            v_n = vel[0]
            result = [
                -v_n * along
                + 0.2 * square * p_bar
                + spread * (0.14 * square - v_n * v_n - 0.5 * sound),
                v_n * plus[1] - 0.4 * v_n * p_bar + plus[0] + along + 0.72 * spread * v_n,
                v_n * plus[2] - vel[1] * (0.4 * p_bar + 0.28 * spread),
                v_n * plus[3] - vel[2] * (0.4 * p_bar + 0.28 * spread),
                plus[4] * v_n + 0.4 * p_bar + 0.28 * spread,
            ]
            for f in range(5):
                val_ref[5 * f + a] = 0.5 * (result[f] - speed * minus[f])
            return carry

        lax.fori_loop(0, 5, body, 0)

    def coarse_sum(table, factor):
        for g in range(25):
            vc_ref[5 * g : 5 * g + 5, :] = val_ref[g, 0:5, 6 * LANES :]
        (summed,) = by_quarter(table, vc_ref[...])
        back = place(summed, ohl_ref[7])
        vc_ref[...] = back
        for g in range(25):
            val_ref[g, :, 5 * LANES : 6 * LANES] = (
                val_ref[g, :, 5 * LANES : 6 * LANES] + factor * vc_ref[5 * g : 5 * g + 8, :]
            )
        vc_ref[120:128, :] = jnp.zeros((8, LANES), F32)

    def spread_faces(scale):
        def body(a, carry):
            for k in range(6):
                d, h = k // 2, k % 2
                lanes = slice(k * LANES, (k + 1) * LANES)
                for f in range(5):
                    base = 200 * FIELD_ORDER[d][f]
                    size = 5 if d == 0 else 8
                    piece = val_ref[5 * f + a, 0:size, lanes]
                    if scale is not None:
                        piece = piece * scale
                    if d == 0:
                        where = pl.ds(base + 40 * a + 4 * h, 5, 8)
                    elif d == 1:
                        where = rows_at(base + 40 * a + 32 * h)
                    else:
                        where = rows_at(base + 160 * h + 8 * a)
                    acc_ref[where, :] = acc_ref[where, :] + piece
            return carry

        lax.fori_loop(0, 5, body, 0)


    diff = basis()[0]

    def slab_along(x, transposed):
        base = 240 if transposed else 0
        total = None
        for m in range(5):
            term = tab_ref[base + 8 * m : base + 8 * m + 8, :] * x[:, m : m + 1, :]
            total = term if total is None else total + term
        return total

    def slab_across(x, transposed):
        matrix = diff.T if transposed else diff
        rows = []
        for k in range(5):
            total = float(matrix[k, 0]) * x[0]
            for m in range(1, 5):
                if matrix[k, m] != 0.0:
                    total = total + float(matrix[k, m]) * x[m]
            rows.append(total[None])
        return jnp.concatenate(rows, axis=0)

    def slab_stack(ref, f, level, transposed):
        base = 280 if transposed else 40
        total = None
        for m in range(5):
            coef = tab_ref[rows_at(base + 40 * level + 8 * m), :]
            term = coef[None] * slab(ref, f, m)
            total = term if total is None else total + term
        return total

    def slab(ref, f, level):
        return ref[rows_at(200 * f + 40 * level, 40), :].reshape(5, 8, LANES)

    def put(ref, f, level, x):
        ref[rows_at(200 * f + 40 * level, 40), :] = x.reshape(40, LANES)

    def volume_forward():
        def first(level, carry):
            s = [slab(u_ref, f, level) for f in range(5)]
            _, vel, _, pressure = primitives(s)
            total = s[4] + pressure

            def flux(d, f):
                if f == 0:
                    return s[d + 1]
                if f == 4:
                    return total * vel[d]
                term = s[f] * vel[d]
                return term + pressure if f == d + 1 else term

            for f in range(5):
                put(fz_ref, f, level, flux(2, f))
                put(
                    acc_ref, f, level,
                    slab_along(flux(0, f), False) + slab_across(flux(1, f), False),
                )
            return carry

        def second(level, carry):
            for f in range(5):
                total = slab(acc_ref, f, level) + slab_stack(fz_ref, f, level, False)
                put(acc_ref, f, level, total * (-met_ref[...])[None])
            return carry

        lax.fori_loop(0, 5, first, 0)
        lax.fori_loop(0, 5, second, 0)

    def volume_adjoint(state_ref, cot_ref, scale):
        def body(level, carry):
            s = [slab(state_ref, f, level) for f in range(5)]
            inv, vel, square, pressure = primitives(s)
            enthalpy = (s[4] + pressure) * inv
            factor = (met_ref[...] * (-scale))[None]
            out = [None] * 5
            p_sum = None
            extra = []

            def add(f, x):
                out[f] = x if out[f] is None else out[f] + x

            for d in range(3):
                w = []
                for f in range(5):
                    if d == 0:
                        w.append(slab_along(slab(cot_ref, f, level), True))
                    elif d == 1:
                        w.append(slab_across(slab(cot_ref, f, level), True))
                    else:
                        w.append(slab_stack(cot_ref, f, level, True))
                p_bar = w[d + 1] + w[4] * vel[d]
                p_sum = p_bar if p_sum is None else p_sum + p_bar
                along = w[1] * vel[0] + w[2] * vel[1] + w[3] * vel[2] + w[4] * enthalpy
                for k in range(3):
                    add(k + 1, vel[d] * w[k + 1])
                extra.append(w[0] + along)
                add(0, -vel[d] * along)
                add(4, w[4] * vel[d])
            add(0, 0.2 * square * p_sum)
            add(4, 0.4 * p_sum)
            for k in range(3):
                add(k + 1, extra[k] - 0.4 * vel[k] * p_sum)
            for f in range(5):
                put(acc_ref, f, level, out[f] * factor)
            return carry

        lax.fori_loop(0, 5, body, 0)


    post(0, u_ref, None)
    post(1, c_ref, 0.5 * STEP)
    volume_forward()
    finish(0, 0)
    face_flux(0)
    coarse_sum(2, -1.0)
    spread_faces(met_ref[...] * (1.0 / W_END))
    for f in range(5):
        at = slice(200 * f, 200 * f + 200)
        u1_ref[at, :] = u_ref[at, :] + STEP * acc_ref[at, :]
    post(2, u1_ref, None)
    volume_adjoint(u1_ref, c_ref, 0.5 * STEP)
    finish(1, 1)
    finish(2, 0)
    face_adjoint(2, 1)
    coarse_sum(3, 1.0)
    spread_faces(None)
    for f in range(5):
        at = slice(200 * f, 200 * f + 200)
        u1_ref[at, :] = 0.5 * c_ref[at, :] + acc_ref[at, :]
    post(3, u1_ref, STEP)
    volume_adjoint(u_ref, u1_ref, STEP)
    finish(3, 1)
    face_adjoint(0, 3)
    coarse_sum(3, 1.0)
    spread_faces(None)
    for f in range(5):
        at = slice(200 * f, 200 * f + 200)
        out_ref[at, :] = (0.5 * c_ref[at, :] + u1_ref[at, :]) + acc_ref[at, :]
    for e in range(4):
        sent_all(e)


def on_device(
    nr, nc, flow_state, cot_final, metric,
    send_col, send_row, exterior, face_kind, mortar_fine, mortar_coarse,
):
    used = nc * COL_ROWS + nr * ROW_ROWS
    send_width = -(-used // LANES) * LANES

    def by_field(x):
        x = x.reshape(25, 5, 5, LANES).transpose(2, 0, 1, 3)
        x = jnp.pad(x, ((0, 0), (0, 0), (0, 3), (0, 0)), constant_values=1.0)
        return x.reshape(1000, LANES)

    none = 768
    slots = jnp.concatenate(
        [
            send_col[0].reshape(nc, 5),
            mortar_fine[0].reshape(4, nc).T,
            jnp.full((nc, COL_ROWS - 9), none, jnp.int32),
        ],
        axis=1,
    ).reshape(-1)
    slots = jnp.concatenate(
        [slots, send_row[0], jnp.full(send_width - used, none, jnp.int32)]
    ).reshape(-1, LANES)
    ext = exterior[0].reshape(6, LANES)
    kind = face_kind[0].reshape(6, LANES)
    col_base, row_base = 768, 768 + 5 * nc
    partner = jnp.array([[k ^ 1] for k in range(6)], jnp.int32) * LANES
    in_col = ext - col_base
    peer = in_col // 5
    row_of = jnp.where(
        ext < col_base,
        ext - partner,
        jnp.where(
            ext < row_base,
            LANES + COL_ROWS * peer + (in_col - 5 * peer),
            LANES + COL_ROWS * nc + (ext - row_base),
        ),
    )
    row_of = jnp.where(kind == 0, row_of, -1)
    lane = np.arange(LANES)
    inside = lane < 4 * nc
    choose = np.stack(
        [
            np.where(inside, COL_ROWS * (lane % nc) + 4, -1000),
            np.where(inside, COL_ROWS * (lane % nc) + 5 + lane // nc, -1000),
        ]
    ).astype(np.int32)
    short = jnp.full(LANES - 4 * nc, none, jnp.int32)
    fine = jnp.concatenate([mortar_fine[0], short])[None]
    coarse = jnp.concatenate([jnp.tile(mortar_coarse[0], 4), short])[None]
    ints = jnp.concatenate([slots, row_of, choose, kind, fine, coarse], axis=0)
    k_high, k_low = mortar_tables()

    vmem = pl.BlockSpec(memory_space=pltpu.VMEM)
    out = pl.pallas_call(
        functools.partial(kernel, nr, nc, send_width),
        out_shape=jax.ShapeDtypeStruct((1000, LANES), F32),
        in_specs=[vmem] * 7,
        out_specs=vmem,
        scratch_shapes=[
            pltpu.VMEM((1000, LANES), F32),
            pltpu.VMEM((1000, LANES), F32),
            pltpu.VMEM((1000, LANES), F32),
            pltpu.VMEM((4, 25, 8, WIDE), F32),
            pltpu.VMEM((4, 25, 8, WIDE), F32),
            pltpu.VMEM((25, 8, WIDE), F32),
            pltpu.VMEM((4, LANES, 768), F32),
            pltpu.VMEM((4, LANES, 8 * LANES), F32),
            pltpu.VMEM((LANES, LANES), F32),
            pltpu.VMEM((768, send_width), BF16),
            pltpu.VMEM((send_width, 768), BF16),
            pltpu.VMEM((8, LANES, LANES), BF16),
            pltpu.VMEM((8, WIDE), F32),
            pltpu.VMEM((4, send_width, LANES), F32),
            pltpu.VMEM((4, send_width, LANES), F32),
            pltpu.SemaphoreType.DMA((4,)),
            pltpu.SemaphoreType.DMA((4,)),
        ],
        compiler_params=pltpu.CompilerParams(
            collective_id=0, has_side_effects=True, vmem_limit_bytes=40 * 2**20
        ),
    )(
        by_field(flow_state),
        by_field(cot_final),
        metric.reshape(1, LANES),
        ints,
        jnp.asarray(stencil_tables()),
        jnp.asarray(k_high),
        jnp.asarray(k_low),
    )
    out = out.reshape(5, 25, 8, LANES)[:, :, :5]
    return out.transpose(1, 2, 0, 3).reshape(125, 5, LANES)


def solution(mesh):
    both = ("row", "col")
    in_specs = (P(None, None, both), P(None, None, both), P(both)) + (P(both, None),) * 6
    return jax.shard_map(
        functools.partial(on_device, mesh.shape["row"], mesh.shape["col"]),
        mesh=mesh,
        in_specs=in_specs,
        out_specs=P(None, None, both),
        check_vma=False,
    )
```

profile of v0, /device:TPU:1, one launch (start us, length us, event | category | flops | bytes accessed | tf_op | source)
XLA Modules:
  0.0 49.4 jit_solution(16523736531954358611)
XLA Ops:
  0.0 0.5 %broadcast.38 = s32[]{:T(128)} broadcast(s32[]{:T(128)} %constant.18.clone.1), dimensions={} | broadcast | bytes 8 | tf_op args[7]
  0.5 0.1 copy-done.12
  0.7 0.7 %reduce.8 = s32[128]{0:T(128)S(1)} reduce(s32[1,128]{1,0:T(1,128)S(1)} %copy-done.12, s32[]{:T(128)} %broadcast.38), dimensions={0}, to_apply=%param.21.reduce_sub_computation.3 | reduce | bytes 1028 | tf_op args[7]
  1.3 0.7 %reduce.9 = s32[160]{0:T(256)S(1)} reduce(s32[1,160]{1,0:T(1,128)S(1)} %copy-done.7, s32[]{:T(128)} %broadcast.38), dimensions={0}, to_apply=%param.17.reduce_sub_computation.3 | reduce | bytes 1284 | tf_op args[3]
  2.0 0.1 pad.14.clone
  2.1 0.1 reshape_squeeze.13
  2.2 0.6 %copy-done.10 = s32[1,32]{1,0:T(1,128)S(1)} copy-done((s32[1,32]{1,0:T(1,128)S(1)}, s32[1,32]{1,0:T(1,128)}, u32[]{:S(2)}) %copy-start.10) | copy-done | bytes 152
  2.8 0.1 broadcast_in_dim_tile.3
  2.9 0.7 %copy-done.6 = s32[1,768]{1,0:T(1,128)S(1)} copy-done((s32[1,768]{1,0:T(1,128)S(1)}, s32[1,768]{1,0:T(1,128)}, u32[]{:S(2)}) %copy-start.6) | copy-done | bytes 3096
  3.6 0.6 %copy-done.11 = s32[6]{0:T(128)S(1)} copy-done((s32[6]{0:T(128)S(1)}, s32[6]{0:T(128)}, u32[]{:S(2)}) %copy-start.11) | copy-done | bytes 48
  4.3 0.1 copy.16
  4.4 0.1 reshape_squeeze.12
  4.5 0.1 add_add_fusion
  4.5 0.1 reshape.32
  4.6 0.7 %copy-done.9 = s32[1,64]{1,0:T(1,128)S(1)} copy-done((s32[1,64]{1,0:T(1,128)S(1)}, s32[1,64]{1,0:T(1,128)}, u32[]{:S(2)}) %copy-start.9) | copy-done | bytes 280
  5.3 0.1 add_bitcast_fusion
  5.4 0.6 %copy-done.8 = s32[2,128]{1,0:T(2,128)S(1)} copy-done((s32[2,128]{1,0:T(2,128)S(1)}, s32[2,128]{1,0:T(2,128)}, u32[]{:S(2)}) %copy-start.8) | copy-done | bytes 1048
  6.0 0.2 concatenate.11.int_ref
  6.1 1.0 %reshape.27 = f32[25,5,5,128]{3,1,0,2:T(8,128)S(1)} reshape(f32[125,5,128]{2,0,1:T(8,128)} %param.14) | data formatting | bytes 640000 | tf_op jit(solution)/shard_map/reshape | solution.py:574
  7.2 0.9 %copy-done.4 = f32[125,5,128]{2,0,1:T(8,128)S(1)} copy-done((f32[125,5,128]{2,0,1:T(8,128)S(1)}, f32[125,5,128]{2,0,1:T(8,128)}, u32[]{:S(2)}) %copy-start.4) | copy-done | bytes 320024
  8.3 0.9 %copy-done.1 = bf16[4,512,128]{2,1,0:T(8,128)(2,1)S(1)} copy-done((bf16[4,512,128]{2,1,0:T(8,128)(2,1)S(1)}, bf16[4,512,128]{2,1,0:T(8,128)(2,1)}, u32[]{:S(2)}) %copy-start.1) | copy-done | bytes 524312
  9.2 0.2 copy-done
  9.4 39.1 %shard_map.136 = f32[1000,128]{1,0:T(8,128)S(1)} custom-call(f32[1000,128]{1,0:T(8,128)S(1)} %bitcast.55, f32[1000,128]{1,0:T(8,128)S(1)} %bitcast.56, f32[1,128]{1,0:T(1,128)S(1)} %bitcast.58, s32[21,128]{1,0:T(8,128)S(1)} %concatenate.11.int_ref, f32[480,128]{1,0:T(8,128)S(1)} %copy-done.2, bf16[4,512,128]{2,1,0:T(8,128)(2,1)S(1)} %copy-done.1, ...), custom_call_target="tpu_custom_call" | custom-call | tf_op jit(solution)/shard_map/pallas_call | solution.py:621
  48.6 0.8 %reshape.35 = f32[125,5,128]{2,0,1:T(8,128)} reshape(f32[25,5,5,128]{3,1,0,2:T(8,128)S(1)} %slice_bitcast_fusion) | data formatting | bytes 640000 | tf_op jit(solution)/shard_map/reshape | solution.py:658
  (27 shorter events, 0.4 us)
Async XLA Ops:
  0.0 0.7 %copy-start.12 = (s32[1,128]{1,0:T(1,128)S(1)}, s32[1,128]{1,0:T(1,128)}, u32[]{:S(2)}) copy-start(s32[1,128]{1,0:T(1,128)} %param.21) | copy-start | bytes 1540
  0.7 0.7 %copy-start.7 = (s32[1,160]{1,0:T(1,128)S(1)}, s32[1,160]{1,0:T(1,128)}, u32[]{:S(2)}) copy-start(s32[1,160]{1,0:T(1,128)} %param.17) | copy-start | bytes 1924
  2.1 0.7 %copy-start.10 = (s32[1,32]{1,0:T(1,128)S(1)}, s32[1,32]{1,0:T(1,128)}, u32[]{:S(2)}) copy-start(s32[1,32]{1,0:T(1,128)} %param.22) | copy-start | bytes 388
  2.2 0.7 %copy-start.5 = (s32[1,768]{1,0:T(1,128)S(1)}, s32[1,768]{1,0:T(1,128)}, u32[]{:S(2)}) copy-start(s32[1,768]{1,0:T(1,128)} %param.20) | copy-start | bytes 9220
  2.9 0.7 %copy-start.6 = (s32[1,768]{1,0:T(1,128)S(1)}, s32[1,768]{1,0:T(1,128)}, u32[]{:S(2)}) copy-start(s32[1,768]{1,0:T(1,128)} %param.19) | copy-start | bytes 9220
  3.6 0.7 %copy-start.11 = (s32[6]{0:T(128)S(1)}, s32[6]{0:T(128)}, u32[]{:S(2)}) copy-start(s32[6]{0:T(128)} %constant.63) | copy-start | bytes 76
  4.6 0.7 %copy-start.9 = (s32[1,64]{1,0:T(1,128)S(1)}, s32[1,64]{1,0:T(1,128)}, u32[]{:S(2)}) copy-start(s32[1,64]{1,0:T(1,128)} %param.18) | copy-start | bytes 772
  5.3 0.7 %copy-start.8 = (s32[2,128]{1,0:T(2,128)S(1)}, s32[2,128]{1,0:T(2,128)}, u32[]{:S(2)}) copy-start(s32[2,128]{1,0:T(2,128)} %constant.44.clone) | copy-start | bytes 3076
  7.2 1.0 %copy-start.4 = (f32[125,5,128]{2,0,1:T(8,128)S(1)}, f32[125,5,128]{2,0,1:T(8,128)}, u32[]{:S(2)}) copy-start(f32[125,5,128]{2,0,1:T(8,128)} %param.15) | copy-start | bytes 960004
  8.1 1.0 %copy-start.1 = (bf16[4,512,128]{2,1,0:T(8,128)(2,1)S(1)}, bf16[4,512,128]{2,1,0:T(8,128)(2,1)}, u32[]{:S(2)}) copy-start(bf16[4,512,128]{2,1,0:T(8,128)(2,1)} %constant.46.clone.khi_ref) | copy-start | bytes 1572868
  8.2 1.2 %copy-start = (bf16[4,512,128]{2,1,0:T(8,128)(2,1)S(1)}, bf16[4,512,128]{2,1,0:T(8,128)(2,1)}, u32[]{:S(2)}) copy-start(bf16[4,512,128]{2,1,0:T(8,128)(2,1)} %constant.47.clone.klo_ref) | copy-start | bytes 1572868
  8.2 1.2 %copy-start.2 = (f32[480,128]{1,0:T(8,128)S(1)}, f32[480,128]{1,0:T(8,128)}, u32[]{:S(2)}) copy-start(f32[480,128]{1,0:T(8,128)} %constant.45.clone.tab_ref) | copy-start | bytes 737284
  8.3 1.1 %copy-start.3 = (f32[128]{0:T(128)S(1)}, f32[128]{0:T(128)}, u32[]{:S(2)}) copy-start(f32[128]{0:T(128)} %param.16) | copy-start | bytes 1540
where the time goes:
time: 49.7 us; the launch traced here: 49.4 us
  Pallas kernels  39.1 us (79%)
  local copies, waits for them, and re-layouts  8.53 us (17%)
  other arithmetic  1.59 us (3%)
    pallas_call x1, Pallas kernels, on_device(): pl.pallas_call(functools.partial(kernel, nr, nc, send_width), out_shape=j...  39.1 us
    unnamed x27, local copies, waits for them, and re-layouts  5.9 us
    unnamed x4, other arithmetic  1.37 us
    reshape x2, local copies, waits for them, and re-layouts, by_field(): x = x.reshape(25, 5, 5, LANES).transpose(2, 0, 1, 3)  1.07 us

commit v1 on v0

--- a/solution.py
+++ b/solution.py
@@ -105,15 +105,39 @@
 
 
 def kernel(
-    nr, nc, send_width,
-    u_ref, c_ref, met_ref, int_ref, tab_ref, khi_ref, klo_ref,
+    nr, nc,
+    u_hbm, c_hbm, met_hbm, col_hbm, row_hbm, ext_hbm, kind_hbm, fine_hbm, coarse_hbm,
+    tab_hbm, khi_hbm, klo_hbm,
     out_ref,
-    u1_ref, acc_ref, fz_ref, own_ref, ext_ref, val_ref, tc_ref, xc_ref, vc_ref,
-    ohs_ref, ohr_ref, ohl_ref, lane_ref,
-    sbuf, rbuf, send_sem, recv_sem,
+    un_ref, cn_ref, met_ref, col_ref, row_ref, exterior_ref, kind_ref, fine_ref, coarse_ref,
+    tab_ref, khi_ref, klo_ref,
+    u_ref, c_ref, u1_ref, acc_ref, fz_ref, own_ref, ext_ref, val_ref, tc_ref, xc_ref, vc_ref,
+    list_ref, ohs_ref, ohr_ref, ohl_ref, lane_ref, slot_ref, came_ref,
+    sbuf, rbuf, load_sem, send_sem, recv_sem,
 ):
     mr = lax.axis_index("row")
     mc = lax.axis_index("col")
+    loads = [
+        pltpu.make_async_copy(src, dst, load_sem.at[n])
+        for n, (src, dst) in enumerate(
+            (
+                (u_hbm, un_ref),
+                (met_hbm, met_ref),
+                (col_hbm, col_ref),
+                (row_hbm, row_ref),
+                (fine_hbm, fine_ref),
+                (coarse_hbm, coarse_ref),
+                (ext_hbm, exterior_ref),
+                (kind_hbm, kind_ref),
+                (c_hbm, cn_ref),
+                (tab_hbm, tab_ref),
+                (khi_hbm, khi_ref),
+                (klo_hbm, klo_ref),
+            )
+        )
+    ]
+    for load in loads:
+        load.start()
     barrier = pltpu.get_barrier_semaphore()
 
     def greet_col(k, carry):
@@ -131,35 +155,73 @@
     lax.fori_loop(1, nc, greet_col, 0)
     lax.fori_loop(1, nr, greet_row, 0)
 
-    chunks = send_width // LANES
-    at_ext = chunks
-    at_sel = at_ext + 6
-    at_kind = at_sel + 2
-    at_fine = at_kind + 6
-    at_coarse = at_fine + 1
-    moved_rows = COL_ROWS * (nc - 1) + ROW_ROWS * (nr - 1)
-
-    def onehot(target, rows, base=0):
-        iota = lax.broadcasted_iota(jnp.int32, (rows, LANES), 0) + base
+    moved_rows = 9 * (nc - 1) + ROW_ROWS * (nr - 1)
+    row_base = COL_ROWS * nc
+
+
+    for e in range(4):
+        tc_ref[e, 120:128, :] = jnp.zeros((8, 768), F32)
+    vc_ref[120:128, :] = jnp.zeros((8, LANES), F32)
+    came_ref[...] = jnp.zeros((4 * LANES, LANES), F32)
+    for load in loads[:8]:
+        load.wait()
+
+    def natural(ref, wide_ref):
+        for g in range(24):
+            for f in range(5):
+                at = 200 * f + 8 * g
+                wide_ref[at : at + 8, :] = ref[f, 5 * g : 5 * g + 8, :]
+        for f in range(5):
+            at = 200 * f + 192
+            wide_ref[at : at + 8, :] = jnp.ones((8, LANES), F32)
+            wide_ref[at : at + 5, :] = ref[f, 120:125, :]
+
+    natural(un_ref, u_ref)
+
+    def onehot(target, base=0):
+        iota = lax.broadcasted_iota(jnp.int32, (LANES, LANES), 0) + base
         return jnp.where(iota == target, 1.0, 0.0).astype(BF16)
 
-    for n in range(chunks):
-        ohs_ref[:, n * LANES : (n + 1) * LANES] = onehot(int_ref[n : n + 1, :], 768)
+    list_ref[...] = jnp.full((1, 5 * LANES), 768, jnp.int32)
+    list_ref[:, 0 : 5 * nc] = col_ref[...]
+    list_ref[:, 2 * LANES : 2 * LANES + 4 * nc] = fine_ref[...]
+    list_ref[:, 3 * LANES : 3 * LANES + 8 * nr] = row_ref[...]
+    for q in range(4):
+        list_ref[:, 4 * LANES + q * nc : 4 * LANES + (q + 1) * nc] = coarse_ref[...]
+
+    def listed(n):
+        return list_ref[:, n * LANES : (n + 1) * LANES]
+
+    coarse_list = listed(4)
+    for n, k in enumerate((0, 1, 5)):
+        for half in range(2):
+            ohs_ref[n * LANES : (n + 1) * LANES, half * LANES : (half + 1) * LANES] = onehot(
+                listed(half), k * LANES
+            )
+    for n, k in enumerate((2, 3)):
+        ohs_ref[(3 + n) * LANES : (4 + n) * LANES, 0:LANES] = onehot(listed(3), k * LANES)
     for k in range(6):
-        target = int_ref[at_ext + k : at_ext + k + 1, :]
-        ohl_ref[k] = onehot(target, LANES)
-        remote = target if k < 4 else int_ref[at_sel + k - 4 : at_sel + k - 3, :] + LANES
-        ohr_ref[:, k * LANES : (k + 1) * LANES] = onehot(remote, send_width, LANES)
-    fine_list = int_ref[at_fine : at_fine + 1, :]
-    coarse_list = int_ref[at_coarse : at_coarse + 1, :]
-    ohl_ref[6] = onehot(fine_list - 512, LANES)
-    ohl_ref[7] = onehot(coarse_list - 640, LANES)
+        lanes = slice(k * LANES, (k + 1) * LANES)
+        at = exterior_ref[:, lanes]
+        near = (kind_ref[:, lanes] == 0) & (at < 768)
+        ohl_ref[k] = onehot(jnp.where(near, at - (k ^ 1) * LANES, -1))
+        far = (kind_ref[:, lanes] == 0) & (at >= 768)
+        half = slice((k % 2) * LANES, (k % 2 + 1) * LANES)
+        if k < 2:
+            at = at - 768
+            peer = (at * 205) >> 10
+            at = (at - 5 * peer) * nc + peer
+            ohr_ref[0:LANES, half] = onehot(jnp.where(far, at, -1))
+        elif k < 4:
+            ohr_ref[LANES:, half] = onehot(jnp.where(far, at - 768 - 5 * nc, -1))
+    ohl_ref[6] = onehot(listed(2), 4 * LANES)
+    ohl_ref[7] = onehot(coarse_list, 5 * LANES)
 
     for k in range(GROUPS):
         lanes = slice(k * LANES, (k + 1) * LANES)
         one = jnp.ones((1, LANES), F32)
         if k < 6:
-            kind = int_ref[at_kind + k : at_kind + k + 1, :]
+            kind = kind_ref[:, lanes]
             rows = [
                 one * (2.0 * (k % 2) - 1.0),
                 jnp.where(kind == 3, -1.0, 1.0),
@@ -167,20 +229,12 @@
                 jnp.where((kind == 0) | (kind == 2), 1.0, 0.0),
                 jnp.where(kind == 1, 1.0, 0.0),
                 one,
-                met_ref[...] * (1.0 / W_END),
             ]
         else:
             valid = jnp.where(coarse_list < 768, 1.0, 0.0)
-            rows = [one, -one, -one, one, 0.0 * one, valid, one]
+            rows = [one, -one, -one, one, 0.0 * one, valid]
         for n, row in enumerate(rows):
             lane_ref[n : n + 1, lanes] = row
-
-    for e in range(4):
-        tc_ref[e, 120:128, :] = jnp.zeros((8, 768), F32)
-        rbuf[e, nc * COL_ROWS + nr * ROW_ROWS :, :] = jnp.zeros(
-            (send_width - nc * COL_ROWS - nr * ROW_ROWS, LANES), F32
-        )
-    vc_ref[120:128, :] = jnp.zeros((8, LANES), F32)
 
 
     def post(e, src_ref, scale):
@@ -205,18 +259,31 @@
         for g in range(25):
             tc_ref[e, 5 * g : 5 * g + 5, :] = own_ref[e, g, 0:5, 0:768]
         both = split_rows(tc_ref[e])
-        sent = dot(both, ohs_ref[...])
-        sent = sent[:LANES] + sent[LANES:]
-        for n in range(chunks):
-            sbuf[e, n * LANES : (n + 1) * LANES, :] = sent[:, n * LANES : (n + 1) * LANES].T
+
+        def group(k, count=1):
+            return both[:, k * LANES : (k + count) * LANES]
+
+        def listed_rows(at, x):
+            x = x[:LANES] + x[LANES:]
+            for n in range(x.shape[1] // LANES):
+                slot_ref[at + n * LANES : at + (n + 1) * LANES, :] = x[:, n * LANES : (n + 1) * LANES].T
+
+        listed_rows(0, dot(group(0, 2), ohs_ref[0:256, :]) + dot(group(5), ohs_ref[256:384, :]))
+        listed_rows(2 * LANES, dot(group(4), ohl_ref[6]))
+        listed_rows(3 * LANES, dot(group(2, 2), ohs_ref[384:640, 0:LANES]))
+        for n in range(5):
+            sbuf[e, pl.ds(n, nc, COL_ROWS), :] = slot_ref[pl.ds(n, nc, 5), :]
+        for q in range(4):
+            sbuf[e, pl.ds(5 + q, nc, COL_ROWS), :] = slot_ref[2 * LANES + q * nc : 2 * LANES + (q + 1) * nc, :]
+        sbuf[e, row_base : row_base + ROW_ROWS * nr, :] = slot_ref[3 * LANES : 3 * LANES + ROW_ROWS * nr, :]
         if e == 0:
             pl.semaphore_wait(barrier, nc + nr - 2)
 
         def push_col(k, carry):
             peer = lax.rem(mc + k, nc)
             pltpu.make_async_remote_copy(
-                src_ref=sbuf.at[e, rows_at(COL_ROWS * peer, COL_ROWS)],
-                dst_ref=rbuf.at[e, rows_at(COL_ROWS * mc, COL_ROWS)],
+                src_ref=sbuf.at[e, rows_at(COL_ROWS * peer, 9)],
+                dst_ref=rbuf.at[e, rows_at(COL_ROWS * mc, 9)],
                 send_sem=send_sem.at[e],
                 recv_sem=recv_sem.at[e],
                 device_id=(mr, peer),
@@ -227,8 +294,8 @@
         def push_row(k, carry):
             peer = lax.rem(mr + k, nr)
             pltpu.make_async_remote_copy(
-                src_ref=sbuf.at[e, rows_at(COL_ROWS * nc + ROW_ROWS * peer, ROW_ROWS)],
-                dst_ref=rbuf.at[e, rows_at(COL_ROWS * nc + ROW_ROWS * mr, ROW_ROWS)],
+                src_ref=sbuf.at[e, rows_at(row_base + ROW_ROWS * peer, ROW_ROWS)],
+                dst_ref=rbuf.at[e, rows_at(row_base + ROW_ROWS * mr, ROW_ROWS)],
                 send_sem=send_sem.at[e],
                 recv_sem=recv_sem.at[e],
                 device_id=(peer, mc),
@@ -240,13 +307,12 @@
         lax.fori_loop(1, nr, push_row, 0)
         own_col = rows_at(COL_ROWS * mc, COL_ROWS)
         rbuf[e, own_col, :] = sbuf[e, own_col, :]
-        own_row = rows_at(COL_ROWS * nc + ROW_ROWS * mr, ROW_ROWS)
+        own_row = rows_at(row_base + ROW_ROWS * mr, ROW_ROWS)
         rbuf[e, own_row, :] = sbuf[e, own_row, :]
         for k in range(6):
-            other = k ^ 1
-            got = dot(both[:, other * LANES : (other + 1) * LANES], ohl_ref[k])
+            got = dot(group(k ^ 1), ohl_ref[k])
             xc_ref[e, :, k * LANES : (k + 1) * LANES] = got[:LANES] + got[LANES:]
-        got = dot(both[:, 5 * LANES : 6 * LANES], ohl_ref[7])
+        got = dot(group(5), ohl_ref[7])
         xc_ref[e, :, 7 * LANES :] = got[:LANES] + got[LANES:]
 
     quarter = lax.broadcasted_iota(jnp.int32, (1, LANES), 1) // nc
@@ -269,15 +335,21 @@
         size = pl.ds(0, moved_rows)
         whole = pltpu.make_async_copy(sbuf.at[e, size], rbuf.at[e, size], recv_sem.at[e])
         whole.wait()
-        came = jnp.concatenate(
-            [rbuf[e, n * LANES : (n + 1) * LANES, :].T for n in range(chunks)], axis=1
-        )
-        got = pick(came, ohr_ref[...])
-        for k in range(4):
-            lanes = slice(k * LANES, (k + 1) * LANES)
-            xc_ref[e, :, lanes] = xc_ref[e, :, lanes] + got[:, lanes]
-        xc_ref[e, :, 6 * LANES : 7 * LANES] = got[:, 5 * LANES :]
-        coarse = jnp.concatenate([got[:, 4 * LANES : 5 * LANES], xc_ref[e, :, 7 * LANES :]], axis=1)
+        for n in range(4):
+            came_ref[n * nc : (n + 1) * nc, :] = rbuf[e, pl.ds(n, nc, COL_ROWS), :]
+        coarse = rbuf[e, pl.ds(4, nc, COL_ROWS), :]
+        for q in range(4):
+            came_ref[LANES + q * nc : LANES + (q + 1) * nc, :] = coarse
+            came_ref[2 * LANES + q * nc : 2 * LANES + (q + 1) * nc, :] = rbuf[
+                e, pl.ds(5 + q, nc, COL_ROWS), :
+            ]
+        came_ref[3 * LANES : 3 * LANES + ROW_ROWS * nr, :] = rbuf[e, row_base : row_base + ROW_ROWS * nr, :]
+        for n, chunk in enumerate((0, 3)):
+            got = pick(came_ref[chunk * LANES : (chunk + 1) * LANES, :].T, ohr_ref[n * LANES : (n + 1) * LANES, :])
+            lanes = slice(2 * n * LANES, 2 * (n + 1) * LANES)
+            xc_ref[e, :, lanes] = xc_ref[e, :, lanes] + got
+        xc_ref[e, :, 6 * LANES : 7 * LANES] = came_ref[2 * LANES : 3 * LANES, :].T
+        coarse = jnp.concatenate([came_ref[LANES : 2 * LANES, :].T, xc_ref[e, :, 7 * LANES :]], axis=1)
         fine_side, coarse_side = by_quarter(table, coarse)
         lanes = slice(4 * LANES, 5 * LANES)
         xc_ref[e, :, lanes] = xc_ref[e, :, lanes] + place(fine_side, ohl_ref[6])
@@ -531,8 +603,13 @@
 
 
     post(0, u_ref, None)
+    loads[8].wait()
+    natural(cn_ref, c_ref)
     post(1, c_ref, 0.5 * STEP)
+    loads[9].wait()
     volume_forward()
+    loads[10].wait()
+    loads[11].wait()
     finish(0, 0)
     face_flux(0)
     coarse_sum(2, -1.0)
@@ -556,9 +633,10 @@
     face_adjoint(0, 3)
     coarse_sum(3, 1.0)
     spread_faces(None)
-    for f in range(5):
-        at = slice(200 * f, 200 * f + 200)
-        out_ref[at, :] = (0.5 * c_ref[at, :] + u1_ref[at, :]) + acc_ref[at, :]
+    for g in range(25):
+        for f in range(5):
+            at = slice(200 * f + 8 * g, 200 * f + 8 * g + 5)
+            out_ref[f, 5 * g : 5 * g + 5, :] = (0.5 * c_ref[at, :] + u1_ref[at, :]) + acc_ref[at, :]
     for e in range(4):
         sent_all(e)
 
@@ -567,95 +645,54 @@
     nr, nc, flow_state, cot_final, metric,
     send_col, send_row, exterior, face_kind, mortar_fine, mortar_coarse,
 ):
-    used = nc * COL_ROWS + nr * ROW_ROWS
-    send_width = -(-used // LANES) * LANES
-
-    def by_field(x):
-        x = x.reshape(25, 5, 5, LANES).transpose(2, 0, 1, 3)
-        x = jnp.pad(x, ((0, 0), (0, 0), (0, 3), (0, 0)), constant_values=1.0)
-        return x.reshape(1000, LANES)
-
-    none = 768
-    slots = jnp.concatenate(
-        [
-            send_col[0].reshape(nc, 5),
-            mortar_fine[0].reshape(4, nc).T,
-            jnp.full((nc, COL_ROWS - 9), none, jnp.int32),
-        ],
-        axis=1,
-    ).reshape(-1)
-    slots = jnp.concatenate(
-        [slots, send_row[0], jnp.full(send_width - used, none, jnp.int32)]
-    ).reshape(-1, LANES)
-    ext = exterior[0].reshape(6, LANES)
-    kind = face_kind[0].reshape(6, LANES)
-    col_base, row_base = 768, 768 + 5 * nc
-    partner = jnp.array([[k ^ 1] for k in range(6)], jnp.int32) * LANES
-    in_col = ext - col_base
-    peer = in_col // 5
-    row_of = jnp.where(
-        ext < col_base,
-        ext - partner,
-        jnp.where(
-            ext < row_base,
-            LANES + COL_ROWS * peer + (in_col - 5 * peer),
-            LANES + COL_ROWS * nc + (ext - row_base),
-        ),
+    k_high, k_low = mortar_tables()
+    operands = (
+        flow_state.transpose(1, 0, 2),
+        cot_final.transpose(1, 0, 2),
+        metric.reshape(1, LANES),
+        send_col,
+        send_row,
+        exterior,
+        face_kind,
+        mortar_fine,
+        mortar_coarse,
+        jnp.asarray(stencil_tables()),
+        jnp.asarray(k_high),
+        jnp.asarray(k_low),
     )
-    row_of = jnp.where(kind == 0, row_of, -1)
-    lane = np.arange(LANES)
-    inside = lane < 4 * nc
-    choose = np.stack(
-        [
-            np.where(inside, COL_ROWS * (lane % nc) + 4, -1000),
-            np.where(inside, COL_ROWS * (lane % nc) + 5 + lane // nc, -1000),
-        ]
-    ).astype(np.int32)
-    short = jnp.full(LANES - 4 * nc, none, jnp.int32)
-    fine = jnp.concatenate([mortar_fine[0], short])[None]
-    coarse = jnp.concatenate([jnp.tile(mortar_coarse[0], 4), short])[None]
-    ints = jnp.concatenate([slots, row_of, choose, kind, fine, coarse], axis=0)
-    k_high, k_low = mortar_tables()
-
-    vmem = pl.BlockSpec(memory_space=pltpu.VMEM)
+    volume = pltpu.VMEM((1000, LANES), F32)
     out = pl.pallas_call(
-        functools.partial(kernel, nr, nc, send_width),
-        out_shape=jax.ShapeDtypeStruct((1000, LANES), F32),
-        in_specs=[vmem] * 7,
-        out_specs=vmem,
-        scratch_shapes=[
-            pltpu.VMEM((1000, LANES), F32),
-            pltpu.VMEM((1000, LANES), F32),
-            pltpu.VMEM((1000, LANES), F32),
+        functools.partial(kernel, nr, nc),
+        out_shape=jax.ShapeDtypeStruct((5, 125, LANES), F32),
+        in_specs=[pl.BlockSpec(memory_space=pl.ANY)] * len(operands),
+        out_specs=pl.BlockSpec(memory_space=pltpu.VMEM),
+        scratch_shapes=[pltpu.VMEM(x.shape, x.dtype) for x in operands]
+        + [volume] * 5
+        + [
             pltpu.VMEM((4, 25, 8, WIDE), F32),
             pltpu.VMEM((4, 25, 8, WIDE), F32),
             pltpu.VMEM((25, 8, WIDE), F32),
             pltpu.VMEM((4, LANES, 768), F32),
             pltpu.VMEM((4, LANES, 8 * LANES), F32),
             pltpu.VMEM((LANES, LANES), F32),
-            pltpu.VMEM((768, send_width), BF16),
-            pltpu.VMEM((send_width, 768), BF16),
+            pltpu.VMEM((1, 5 * LANES), jnp.int32),
+            pltpu.VMEM((5 * LANES, 2 * LANES), BF16),
+            pltpu.VMEM((2 * LANES, 2 * LANES), BF16),
             pltpu.VMEM((8, LANES, LANES), BF16),
             pltpu.VMEM((8, WIDE), F32),
-            pltpu.VMEM((4, send_width, LANES), F32),
-            pltpu.VMEM((4, send_width, LANES), F32),
+            pltpu.VMEM((4 * LANES, LANES), F32),
+            pltpu.VMEM((4 * LANES, LANES), F32),
+            pltpu.VMEM((4, COL_ROWS * nc + ROW_ROWS * nr, LANES), F32),
+            pltpu.VMEM((4, COL_ROWS * nc + ROW_ROWS * nr, LANES), F32),
+            pltpu.SemaphoreType.DMA((len(operands),)),
             pltpu.SemaphoreType.DMA((4,)),
             pltpu.SemaphoreType.DMA((4,)),
         ],
         compiler_params=pltpu.CompilerParams(
-            collective_id=0, has_side_effects=True, vmem_limit_bytes=40 * 2**20
+            collective_id=0, has_side_effects=True, vmem_limit_bytes=56 * 2**20
         ),
-    )(
-        by_field(flow_state),
-        by_field(cot_final),
-        metric.reshape(1, LANES),
-        ints,
-        jnp.asarray(stencil_tables()),
-        jnp.asarray(k_high),
-        jnp.asarray(k_low),
-    )
-    out = out.reshape(5, 25, 8, LANES)[:, :, :5]
-    return out.transpose(1, 2, 0, 3).reshape(125, 5, LANES)
+    )(*operands)
+    return out.transpose(1, 0, 2)
 
 
 def solution(mesh):

time: 49.7 us -> 37.7 us (0.76)
  local copies, waits for them, and re-layouts: 8.53 us -> 1.72 us
  Pallas kernels: 39.1 us -> 35.9 us
  other arithmetic: 1.59 us -> 0 us
    unnamed x27 -> x1, local copies, waits for them, and re-layouts: 5.9 us -> 1.72 us
    pallas_call x1, Pallas kernels: 39.1 us -> 35.9 us  [on_device(): pl.pallas_call(functools.partial(kernel, nr, nc), out_shape=jax.ShapeDtyp...]
    reshape x4 -> x0, local copies, waits for them, and re-layouts: 1.92 us -> none  [the longest x2 1.07 us: by_field(): x = x.reshape(25, 5, 5, LANES).transpose(2, 0, 1, 3)]
    unnamed x4 -> x0, other arithmetic: 1.37 us -> none
where the time goes in v1:
time: 37.7 us; the launch traced here: 37.6 us
  Pallas kernels  35.9 us (95%)
  local copies, waits for them, and re-layouts  1.72 us (5%)
    pallas_call x1, Pallas kernels, on_device(): pl.pallas_call(functools.partial(kernel, nr, nc), out_shape=jax.ShapeDtyp...  35.9 us
    unnamed x1, local copies, waits for them, and re-layouts  1.72 us

profile of v1, /device:TPU:1, one launch (start us, length us, event | category | flops | bytes accessed | tf_op | source)
XLA Modules:
  0.0 37.6 jit_solution(9189378716487566576)
XLA Ops:
  0.0 35.9 %shard_map.118 = f32[5,125,128]{2,1,0:T(8,128)} custom-call(f32[5,125,128]{2,1,0:T(8,128)} %bitcast.5, f32[5,125,128]{2,1,0:T(8,128)} %bitcast.6, f32[1,128]{1,0:T(1,128)} %bitcast.7, s32[1,160]{1,0:T(1,128)} %col_hbm.1, s32[1,64]{1,0:T(1,128)} %row_hbm.1, s32[1,768]{1,0:T(1,128)} %ext_hbm.1, s32[1,768]{1,0:T(1,128)} %kind_hbm.1, s32[1,128]{1,0:T(1,128)} %fine_hbm.1, ...), custom_call_target="tpu_custom_call" | custom-call | tf_op jit(solution)/shard_map/pallas_call | solution.py:664
  35.9 1.7 %copy.14 = f32[125,5,128]{2,0,1:T(8,128)} copy(f32[125,5,128]{2,0,1:T(8,128)} %bitcast.4) | data formatting | bytes 640000

commit v2 on v1

--- a/solution.py
+++ b/solution.py
@@ -12,6 +12,7 @@
 STEP = 0.005
 W_END = 0.1
 COL_ROWS = 16
+COL_SENT = 9
 ROW_ROWS = 8
 LANES = 128
 GROUPS = 7
@@ -100,6 +101,21 @@
     return both[: x.shape[0]] + both[x.shape[0] :]
 
 
+def col_offsets(nc):
+    if nc != 32:
+        return list(range(1, nc))
+    every = [(y, x, c) for y in range(4) for x in range(4) for c in range(2)]
+    return sorted(every[1:], key=lambda o: (-(2 - abs(o[0] - 2)) - (2 - abs(o[1] - 2)), o))
+
+
+def col_peer(me, away, nc):
+    if nc != 32:
+        return lax.rem(me + away, nc)
+    y, x, core = me // 8, lax.rem(me // 2, 4), lax.rem(me, 2)
+    y, x, core = lax.rem(y + away[0], 4), lax.rem(x + away[1], 4), lax.rem(core + away[2], 2)
+    return 8 * y + 2 * x + core
+
+
 def rows_at(start, size=8):
     return pl.ds(pl.multiple_of(start, 8), size)
 
@@ -108,12 +124,12 @@
     nr, nc,
     u_hbm, c_hbm, met_hbm, col_hbm, row_hbm, ext_hbm, kind_hbm, fine_hbm, coarse_hbm,
     tab_hbm, khi_hbm, klo_hbm,
-    out_ref,
+    out_hbm,
     un_ref, cn_ref, met_ref, col_ref, row_ref, exterior_ref, kind_ref, fine_ref, coarse_ref,
     tab_ref, khi_ref, klo_ref,
     u_ref, c_ref, u1_ref, acc_ref, fz_ref, own_ref, ext_ref, val_ref, tc_ref, xc_ref, vc_ref,
-    list_ref, ohs_ref, ohr_ref, ohl_ref, lane_ref, slot_ref, came_ref,
-    sbuf, rbuf, load_sem, send_sem, recv_sem,
+    term_ref, out_ref, list_ref, ohs_ref, ohr_ref, ohl_ref, lane_ref, slot_ref, came_ref,
+    sbuf, rbuf, load_sem, send_sem, recv_sem, out_sem,
 ):
     mr = lax.axis_index("row")
     mc = lax.axis_index("col")
@@ -155,15 +171,13 @@
     lax.fori_loop(1, nc, greet_col, 0)
     lax.fori_loop(1, nr, greet_row, 0)
 
-    moved_rows = 9 * (nc - 1) + ROW_ROWS * (nr - 1)
+    moved_rows = COL_SENT * (nc - 1) + ROW_ROWS * (nr - 1)
     row_base = COL_ROWS * nc
 
 
     for e in range(4):
         tc_ref[e, 120:128, :] = jnp.zeros((8, 768), F32)
-    vc_ref[120:128, :] = jnp.zeros((8, LANES), F32)
-    came_ref[...] = jnp.zeros((4 * LANES, LANES), F32)
-    for load in loads[:8]:
+    for load in loads[2:6]:
         load.wait()
 
     def natural(ref, wide_ref):
@@ -176,8 +190,6 @@
             wide_ref[at : at + 8, :] = jnp.ones((8, LANES), F32)
             wide_ref[at : at + 5, :] = ref[f, 120:125, :]
 
-    natural(un_ref, u_ref)
-
     def onehot(target, base=0):
         iota = lax.broadcasted_iota(jnp.int32, (LANES, LANES), 0) + base
         return jnp.where(iota == target, 1.0, 0.0).astype(BF16)
@@ -200,41 +212,50 @@
             )
     for n, k in enumerate((2, 3)):
         ohs_ref[(3 + n) * LANES : (4 + n) * LANES, 0:LANES] = onehot(listed(3), k * LANES)
-    for k in range(6):
-        lanes = slice(k * LANES, (k + 1) * LANES)
-        at = exterior_ref[:, lanes]
-        near = (kind_ref[:, lanes] == 0) & (at < 768)
-        ohl_ref[k] = onehot(jnp.where(near, at - (k ^ 1) * LANES, -1))
-        far = (kind_ref[:, lanes] == 0) & (at >= 768)
-        half = slice((k % 2) * LANES, (k % 2 + 1) * LANES)
-        if k < 2:
-            at = at - 768
-            peer = (at * 205) >> 10
-            at = (at - 5 * peer) * nc + peer
-            ohr_ref[0:LANES, half] = onehot(jnp.where(far, at, -1))
-        elif k < 4:
-            ohr_ref[LANES:, half] = onehot(jnp.where(far, at - 768 - 5 * nc, -1))
     ohl_ref[6] = onehot(listed(2), 4 * LANES)
     ohl_ref[7] = onehot(coarse_list, 5 * LANES)
 
-    for k in range(GROUPS):
-        lanes = slice(k * LANES, (k + 1) * LANES)
-        one = jnp.ones((1, LANES), F32)
-        if k < 6:
-            kind = kind_ref[:, lanes]
-            rows = [
-                one * (2.0 * (k % 2) - 1.0),
-                jnp.where(kind == 3, -1.0, 1.0),
-                one,
-                jnp.where((kind == 0) | (kind == 2), 1.0, 0.0),
-                jnp.where(kind == 1, 1.0, 0.0),
-                one,
-            ]
-        else:
-            valid = jnp.where(coarse_list < 768, 1.0, 0.0)
-            rows = [one, -one, -one, one, 0.0 * one, valid]
-        for n, row in enumerate(rows):
-            lane_ref[n : n + 1, lanes] = row
+    loads[0].wait()
+    natural(un_ref, u_ref)
+
+    def receive_tables():
+        vc_ref[120:128, :] = jnp.zeros((8, LANES), F32)
+        came_ref[...] = jnp.zeros((4 * LANES, LANES), F32)
+        loads[1].wait()
+        loads[6].wait()
+        loads[7].wait()
+        for k in range(6):
+            lanes = slice(k * LANES, (k + 1) * LANES)
+            at = exterior_ref[:, lanes]
+            near = (kind_ref[:, lanes] == 0) & (at < 768)
+            ohl_ref[k] = onehot(jnp.where(near, at - (k ^ 1) * LANES, -1))
+            far = (kind_ref[:, lanes] == 0) & (at >= 768)
+            half = slice((k % 2) * LANES, (k % 2 + 1) * LANES)
+            if k < 2:
+                at = at - 768
+                peer = (at * 205) >> 10
+                at = (at - 5 * peer) * nc + peer
+                ohr_ref[0:LANES, half] = onehot(jnp.where(far, at, -1))
+            elif k < 4:
+                ohr_ref[LANES:, half] = onehot(jnp.where(far, at - 768 - 5 * nc, -1))
+        for k in range(GROUPS):
+            lanes = slice(k * LANES, (k + 1) * LANES)
+            one = jnp.ones((1, LANES), F32)
+            if k < 6:
+                kind = kind_ref[:, lanes]
+                rows = [
+                    one * (2.0 * (k % 2) - 1.0),
+                    jnp.where(kind == 3, -1.0, 1.0),
+                    one,
+                    jnp.where((kind == 0) | (kind == 2), 1.0, 0.0),
+                    jnp.where(kind == 1, 1.0, 0.0),
+                    one,
+                ]
+            else:
+                valid = jnp.where(coarse_list < 768, 1.0, 0.0)
+                rows = [one, -one, -one, one, 0.0 * one, valid]
+            for n, row in enumerate(rows):
+                lane_ref[n : n + 1, lanes] = row
 
 
     def post(e, src_ref, scale):
@@ -279,20 +300,18 @@
         if e == 0:
             pl.semaphore_wait(barrier, nc + nr - 2)
 
-        def push_col(k, carry):
-            peer = lax.rem(mc + k, nc)
+        for away in col_offsets(nc):
+            peer = col_peer(mc, away, nc)
             pltpu.make_async_remote_copy(
-                src_ref=sbuf.at[e, rows_at(COL_ROWS * peer, 9)],
-                dst_ref=rbuf.at[e, rows_at(COL_ROWS * mc, 9)],
+                src_ref=sbuf.at[e, rows_at(COL_ROWS * peer, COL_SENT)],
+                dst_ref=rbuf.at[e, rows_at(COL_ROWS * mc, COL_SENT)],
                 send_sem=send_sem.at[e],
                 recv_sem=recv_sem.at[e],
                 device_id=(mr, peer),
                 device_id_type=MESH,
             ).start()
-            return carry
-
-        def push_row(k, carry):
-            peer = lax.rem(mr + k, nr)
+        for away in sorted(range(1, nr), key=lambda k: -min(k, nr - k)):
+            peer = lax.rem(mr + away, nr)
             pltpu.make_async_remote_copy(
                 src_ref=sbuf.at[e, rows_at(row_base + ROW_ROWS * peer, ROW_ROWS)],
                 dst_ref=rbuf.at[e, rows_at(row_base + ROW_ROWS * mr, ROW_ROWS)],
@@ -301,35 +320,34 @@
                 device_id=(peer, mc),
                 device_id_type=MESH,
             ).start()
-            return carry
-
-        lax.fori_loop(1, nc, push_col, 0)
-        lax.fori_loop(1, nr, push_row, 0)
         own_col = rows_at(COL_ROWS * mc, COL_ROWS)
         rbuf[e, own_col, :] = sbuf[e, own_col, :]
         own_row = rows_at(row_base + ROW_ROWS * mr, ROW_ROWS)
         rbuf[e, own_row, :] = sbuf[e, own_row, :]
+    quarter = lax.broadcasted_iota(jnp.int32, (1, LANES), 1) // nc
+
+    def by_quarter(at, x):
+        hi, lo = split(x)
+        k_hi, k_lo = khi_ref[at], klo_ref[at]
+        full = dot(k_hi, hi) + (dot(k_lo, hi) + dot(k_hi, lo))
+        total = jnp.where(quarter == 0, full[:LANES], 0.0)
+        for q in range(1, 4):
+            total = jnp.where(quarter == q, full[q * LANES : (q + 1) * LANES], total)
+        return total
+
+    def near(e, table):
+        both = split_rows(tc_ref[e])
+
+        def group(k):
+            return both[:, k * LANES : (k + 1) * LANES]
+
         for k in range(6):
             got = dot(group(k ^ 1), ohl_ref[k])
             xc_ref[e, :, k * LANES : (k + 1) * LANES] = got[:LANES] + got[LANES:]
         got = dot(group(5), ohl_ref[7])
-        xc_ref[e, :, 7 * LANES :] = got[:LANES] + got[LANES:]
-
-    quarter = lax.broadcasted_iota(jnp.int32, (1, LANES), 1) // nc
-
-    def by_quarter(at, x):
-        width = x.shape[1] // LANES
-        hi, lo = split(x)
-        k_hi, k_lo = khi_ref[at], klo_ref[at]
-        full = dot(k_hi, hi) + (dot(k_lo, hi) + dot(k_hi, lo))
-        out = []
-        for n in range(width):
-            total = jnp.zeros((LANES, LANES), F32)
-            for q in range(4):
-                block = full[q * LANES : (q + 1) * LANES, n * LANES : (n + 1) * LANES]
-                total = total + jnp.where(quarter == q, block, 0.0)
-            out.append(total)
-        return out
+        xc_ref[e, :, 7 * LANES :] = by_quarter(table, got[:LANES] + got[LANES:])
+        for g in range(25):
+            own_ref[e, g, :, 6 * LANES :] = xc_ref[e, 5 * g : 5 * g + 8, WIDE:]
 
     def finish(e, table):
         size = pl.ds(0, moved_rows)
@@ -349,14 +367,11 @@
             lanes = slice(2 * n * LANES, 2 * (n + 1) * LANES)
             xc_ref[e, :, lanes] = xc_ref[e, :, lanes] + got
         xc_ref[e, :, 6 * LANES : 7 * LANES] = came_ref[2 * LANES : 3 * LANES, :].T
-        coarse = jnp.concatenate([came_ref[LANES : 2 * LANES, :].T, xc_ref[e, :, 7 * LANES :]], axis=1)
-        fine_side, coarse_side = by_quarter(table, coarse)
+        fine_side = by_quarter(table, came_ref[LANES : 2 * LANES, :].T)
         lanes = slice(4 * LANES, 5 * LANES)
         xc_ref[e, :, lanes] = xc_ref[e, :, lanes] + place(fine_side, ohl_ref[6])
-        xc_ref[e, :, 7 * LANES :] = coarse_side
         for g in range(25):
             ext_ref[e, g] = xc_ref[e, 5 * g : 5 * g + 8, 0:WIDE]
-            own_ref[e, g, :, 6 * LANES :] = xc_ref[e, 5 * g : 5 * g + 8, WIDE:]
 
     def sent_all(e):
         size = pl.ds(0, moved_rows)
@@ -417,9 +432,39 @@
 
         lax.fori_loop(0, 5, body, 0)
 
+    def terms_of(state, a):
+        own, ext = fill_states(state, a)
+        inv, vel, square, pressure = primitives(own)
+        inv_b, vel_b, _, pressure_b = primitives(ext)
+        sound = 1.4 * pressure * inv
+        speed = jnp.sqrt(
+            0.5 * (vel[0] * vel[0] + vel_b[0] * vel_b[0] + sound + 1.4 * pressure_b * inv_b)
+        )
+        return [
+            *vel,
+            (own[4] + pressure) * inv,
+            0.2 * square,
+            0.14 * square - vel[0] * vel[0] - 0.5 * sound,
+            speed,
+            0.5 * inv / speed,
+            *[ext[f] - own[f] for f in range(5)],
+        ]
+
+    def face_terms(state):
+        def body(a, carry):
+            for n, term in enumerate(terms_of(state, a)):
+                term_ref[n, a] = term
+            return carry
+
+        lax.fori_loop(0, 5, body, 0)
+
     def face_adjoint(state, cot):
         def body(a, carry):
-            own, ext = fill_states(state, a)
+            if state is None:
+                terms = [term_ref[n, a] for n in range(13)]
+            else:
+                terms = terms_of(state, a)
+            v_n, v_1, v_2, enthalpy, fifth, of_density, speed, half_over, *gap = terms
             y, y_ext = both_states(cot, a)
             gathered = lane_row(3) > 0.5
             flip = 1.0 - 2.0 * lane_row(4)
@@ -427,31 +472,21 @@
                 jnp.where(gathered, y_ext[f], y[f] * flip if f == 1 else y[f]) for f in range(5)
             ]
             orient, sign = lane_row(0), lane_row(2)
-            inv, vel, square, pressure = primitives(own)
-            inv_b, vel_b, _, pressure_b = primitives(ext)
-            sound = 1.4 * pressure * inv
-            speed2 = 0.5 * (
-                vel[0] * vel[0] + vel_b[0] * vel_b[0] + sound + 1.4 * pressure_b * inv_b
-            )
-            speed = jnp.sqrt(speed2)
             plus = [orient * (y_ext[f] + sign * y[f]) for f in range(5)]
             minus = [y[f] - y_ext[f] for f in range(5)]
-            dots = minus[0] * (ext[0] - own[0])
+            dots = minus[0] * gap[0]
             for f in range(1, 5):
-                dots = dots + minus[f] * (ext[f] - own[f])
-            spread = 0.5 * dots * inv / speed
-            p_bar = plus[1] + plus[4] * vel[0]
-            along = plus[1] * vel[0] + plus[2] * vel[1] + plus[3] * vel[2]
-            along = along + plus[4] * (own[4] + pressure) * inv
-            v_n = vel[0]
+                dots = dots + minus[f] * gap[f]
+            spread = dots * half_over
+            p_bar = plus[1] + plus[4] * v_n
+            along = plus[1] * v_n + plus[2] * v_1 + plus[3] * v_2 + plus[4] * enthalpy
+            side = 0.4 * p_bar + 0.28 * spread
             result = [
-                -v_n * along
-                + 0.2 * square * p_bar
-                + spread * (0.14 * square - v_n * v_n - 0.5 * sound),
-                v_n * plus[1] - 0.4 * v_n * p_bar + plus[0] + along + 0.72 * spread * v_n,
-                v_n * plus[2] - vel[1] * (0.4 * p_bar + 0.28 * spread),
-                v_n * plus[3] - vel[2] * (0.4 * p_bar + 0.28 * spread),
-                plus[4] * v_n + 0.4 * p_bar + 0.28 * spread,
+                fifth * p_bar - v_n * along + spread * of_density,
+                v_n * (plus[1] - 0.4 * p_bar + 0.72 * spread) + plus[0] + along,
+                v_n * plus[2] - v_1 * side,
+                v_n * plus[3] - v_2 * side,
+                plus[4] * v_n + side,
             ]
             for f in range(5):
                 val_ref[5 * f + a] = 0.5 * (result[f] - speed * minus[f])
@@ -462,8 +497,7 @@
     def coarse_sum(table, factor):
         for g in range(25):
             vc_ref[5 * g : 5 * g + 5, :] = val_ref[g, 0:5, 6 * LANES :]
-        (summed,) = by_quarter(table, vc_ref[...])
-        back = place(summed, ohl_ref[7])
+        back = place(by_quarter(table, vc_ref[...]), ohl_ref[7])
         vc_ref[...] = back
         for g in range(25):
             val_ref[g, :, 5 * LANES : 6 * LANES] = (
@@ -603,13 +637,14 @@
 
 
     post(0, u_ref, None)
+    receive_tables()
     loads[8].wait()
     natural(cn_ref, c_ref)
     post(1, c_ref, 0.5 * STEP)
-    loads[9].wait()
+    for load in loads[9:]:
+        load.wait()
+    near(0, 0)
     volume_forward()
-    loads[10].wait()
-    loads[11].wait()
     finish(0, 0)
     face_flux(0)
     coarse_sum(2, -1.0)
@@ -618,8 +653,10 @@
         at = slice(200 * f, 200 * f + 200)
         u1_ref[at, :] = u_ref[at, :] + STEP * acc_ref[at, :]
     post(2, u1_ref, None)
+    near(2, 0)
+    near(1, 1)
+    finish(1, 1)
     volume_adjoint(u1_ref, c_ref, 0.5 * STEP)
-    finish(1, 1)
     finish(2, 0)
     face_adjoint(2, 1)
     coarse_sum(3, 1.0)
@@ -628,17 +665,24 @@
         at = slice(200 * f, 200 * f + 200)
         u1_ref[at, :] = 0.5 * c_ref[at, :] + acc_ref[at, :]
     post(3, u1_ref, STEP)
+    near(3, 1)
+    face_terms(0)
     volume_adjoint(u_ref, u1_ref, STEP)
     finish(3, 1)
-    face_adjoint(0, 3)
+    face_adjoint(None, 3)
     coarse_sum(3, 1.0)
     spread_faces(None)
-    for g in range(25):
-        for f in range(5):
+    stores = []
+    for f in range(5):
+        for g in range(25):
             at = slice(200 * f + 8 * g, 200 * f + 8 * g + 5)
-            out_ref[f, 5 * g : 5 * g + 5, :] = (0.5 * c_ref[at, :] + u1_ref[at, :]) + acc_ref[at, :]
+            out_ref[f, 5 * g : 5 * g + 5, :] = u1_ref[at, :] + acc_ref[at, :]
+        stores.append(pltpu.make_async_copy(out_ref.at[f], out_hbm.at[f], out_sem.at[f]))
+        stores[f].start()
     for e in range(4):
         sent_all(e)
+    for store in stores:
+        store.wait()
 
 
 def on_device(
@@ -665,7 +709,7 @@
         functools.partial(kernel, nr, nc),
         out_shape=jax.ShapeDtypeStruct((5, 125, LANES), F32),
         in_specs=[pl.BlockSpec(memory_space=pl.ANY)] * len(operands),
-        out_specs=pl.BlockSpec(memory_space=pltpu.VMEM),
+        out_specs=pl.BlockSpec(memory_space=pl.ANY),
         scratch_shapes=[pltpu.VMEM(x.shape, x.dtype) for x in operands]
         + [volume] * 5
         + [
@@ -675,6 +719,8 @@
             pltpu.VMEM((4, LANES, 768), F32),
             pltpu.VMEM((4, LANES, 8 * LANES), F32),
             pltpu.VMEM((LANES, LANES), F32),
+            pltpu.VMEM((13, 5, 8, WIDE), F32),
+            pltpu.VMEM((5, 125, LANES), F32),
             pltpu.VMEM((1, 5 * LANES), jnp.int32),
             pltpu.VMEM((5 * LANES, 2 * LANES), BF16),
             pltpu.VMEM((2 * LANES, 2 * LANES), BF16),
@@ -687,12 +733,13 @@
             pltpu.SemaphoreType.DMA((len(operands),)),
             pltpu.SemaphoreType.DMA((4,)),
             pltpu.SemaphoreType.DMA((4,)),
+            pltpu.SemaphoreType.DMA((5,)),
         ],
         compiler_params=pltpu.CompilerParams(
             collective_id=0, has_side_effects=True, vmem_limit_bytes=56 * 2**20
         ),
     )(*operands)
-    return out.transpose(1, 0, 2)
+    return 0.5 * cot_final + out.transpose(1, 0, 2)
 
 
 def solution(mesh):

time: 37.7 us -> 35.8 us (0.950)
  Pallas kernels: 35.9 us -> 33.9 us
  other arithmetic: 0 us -> 1.73 us
  local copies, waits for them, and re-layouts: 1.72 us -> 0.01 us
    pallas_call x1, Pallas kernels: 35.9 us -> 33.9 us  [on_device(): pl.pallas_call(functools.partial(kernel, nr, nc), out_shape=jax.ShapeDtyp...]
    add x0 -> x1, other arithmetic: none -> 1.73 us  [on_device(): return 0.5 * cot_final + out.transpose(1, 0, 2)]
    unnamed x1 -> x2, local copies, waits for them, and re-layouts: 1.72 us -> 0.01 us
where the time goes in v2:
time: 35.8 us; the launch traced here: 35.6 us
  Pallas kernels  33.9 us (95%)
  other arithmetic  1.73 us (5%)
    pallas_call x1, Pallas kernels, on_device(): pl.pallas_call(functools.partial(kernel, nr, nc), out_shape=jax.ShapeDtyp...  33.9 us
    add x1, other arithmetic, on_device(): return 0.5 * cot_final + out.transpose(1, 0, 2)  1.73 us

profile of v2, /device:TPU:1, one launch (start us, length us, event | category | flops | bytes accessed | tf_op | source)
XLA Modules:
  0.0 35.6 jit_solution(443885879445979057)
XLA Ops:
  0.0 0.0 copy-start
  0.0 33.9 %shard_map.118 = f32[5,125,128]{2,1,0:T(8,128)} custom-call(f32[5,125,128]{2,1,0:T(8,128)} %bitcast.6, f32[5,125,128]{2,1,0:T(8,128)} %bitcast.5, f32[1,128]{1,0:T(1,128)} %bitcast.7, s32[1,160]{1,0:T(1,128)} %col_hbm.1, s32[1,64]{1,0:T(1,128)} %row_hbm.1, s32[1,768]{1,0:T(1,128)} %ext_hbm.1, s32[1,768]{1,0:T(1,128)} %kind_hbm.1, s32[1,128]{1,0:T(1,128)} %fine_hbm.1, ...), custom_call_target="tpu_custom_call" | custom-call | tf_op jit(solution)/shard_map/pallas_call | solution.py:708
  33.9 0.0 copy-done
  33.9 1.7 %bitcast_add_fusion = f32[125,5,128]{2,0,1:T(8,128)} fusion(f32[5,125,128]{2,1,0:T(8,128)} %shard_map.118, f32[125,5,128]{2,0,1:T(8,128)S(1)} %copy-done), kind=kLoop, calls=%fused_computation | loop fusion | flops 160000 | bytes 960000 | tf_op jit(solution)/shard_map/add | solution.py:742
Async XLA Ops:
  0.0 33.9 %copy-start = (f32[125,5,128]{2,0,1:T(8,128)S(1)}, f32[125,5,128]{2,0,1:T(8,128)}, u32[]{:S(2)}) copy-start(f32[125,5,128]{2,0,1:T(8,128)} %param.13) | copy-start | bytes 960004

commit v3 on v2

--- a/solution.py
+++ b/solution.py
@@ -276,7 +276,7 @@
                     own_ref[e, 5 * f + a, : piece.shape[0], lanes] = piece
             return carry
 
-        lax.fori_loop(0, 5, take, 0)
+        lax.fori_loop(0, 5, take, 0, unroll=True)
         for g in range(25):
             tc_ref[e, 5 * g : 5 * g + 5, :] = own_ref[e, g, 0:5, 0:768]
         both = split_rows(tc_ref[e])
@@ -430,7 +430,7 @@
                 )
             return carry
 
-        lax.fori_loop(0, 5, body, 0)
+        lax.fori_loop(0, 5, body, 0, unroll=True)
 
     def terms_of(state, a):
         own, ext = fill_states(state, a)
@@ -456,7 +456,7 @@
                 term_ref[n, a] = term
             return carry
 
-        lax.fori_loop(0, 5, body, 0)
+        lax.fori_loop(0, 5, body, 0, unroll=True)
 
     def face_adjoint(state, cot):
         def body(a, carry):
@@ -492,7 +492,7 @@
                 val_ref[5 * f + a] = 0.5 * (result[f] - speed * minus[f])
             return carry
 
-        lax.fori_loop(0, 5, body, 0)
+        lax.fori_loop(0, 5, body, 0, unroll=True)
 
     def coarse_sum(table, factor):
         for g in range(25):
@@ -525,7 +525,7 @@
                     acc_ref[where, :] = acc_ref[where, :] + piece
             return carry
 
-        lax.fori_loop(0, 5, body, 0)
+        lax.fori_loop(0, 5, body, 0, unroll=True)
 
 
     diff = basis()[0]

time: 35.8 us -> 33.5 us (0.936)
  Pallas kernels: 33.9 us -> 31.7 us
    pallas_call x1, Pallas kernels: 33.9 us -> 31.7 us  [on_device(): pl.pallas_call(functools.partial(kernel, nr, nc), out_shape=jax.ShapeDtyp...]
where the time goes in v3:
time: 33.5 us; the launch traced here: 33.4 us
  Pallas kernels  31.7 us (95%)
  other arithmetic  1.73 us (5%)
    pallas_call x1, Pallas kernels, on_device(): pl.pallas_call(functools.partial(kernel, nr, nc), out_shape=jax.ShapeDtyp...  31.7 us
    add x1, other arithmetic, on_device(): return 0.5 * cot_final + out.transpose(1, 0, 2)  1.73 us

profile of v3, /device:TPU:1, one launch (start us, length us, event | category | flops | bytes accessed | tf_op | source)
XLA Modules:
  0.0 33.4 jit_solution(16002385218798339827)
XLA Ops:
  0.0 0.0 copy-start
  0.0 31.7 %shard_map.118 = f32[5,125,128]{2,1,0:T(8,128)} custom-call(f32[5,125,128]{2,1,0:T(8,128)} %bitcast.6, f32[5,125,128]{2,1,0:T(8,128)} %bitcast.5, f32[1,128]{1,0:T(1,128)} %bitcast.7, s32[1,160]{1,0:T(1,128)} %col_hbm.1, s32[1,64]{1,0:T(1,128)} %row_hbm.1, s32[1,768]{1,0:T(1,128)} %ext_hbm.1, s32[1,768]{1,0:T(1,128)} %kind_hbm.1, s32[1,128]{1,0:T(1,128)} %fine_hbm.1, ...), custom_call_target="tpu_custom_call" | custom-call | tf_op jit(solution)/shard_map/pallas_call | solution.py:708
  31.7 0.0 copy-done
  31.7 1.7 %bitcast_add_fusion = f32[125,5,128]{2,0,1:T(8,128)} fusion(f32[5,125,128]{2,1,0:T(8,128)} %shard_map.118, f32[125,5,128]{2,0,1:T(8,128)S(1)} %copy-done), kind=kLoop, calls=%fused_computation | loop fusion | flops 160000 | bytes 960000 | tf_op jit(solution)/shard_map/add | solution.py:742
Async XLA Ops:
  0.0 31.7 %copy-start = (f32[125,5,128]{2,0,1:T(8,128)S(1)}, f32[125,5,128]{2,0,1:T(8,128)}, u32[]{:S(2)}) copy-start(f32[125,5,128]{2,0,1:T(8,128)} %param.13) | copy-start | bytes 960004

commit v4 on v3

--- a/solution.py
+++ b/solution.py
@@ -106,6 +106,10 @@
         return list(range(1, nc))
     every = [(y, x, c) for y in range(4) for x in range(4) for c in range(2)]
     return sorted(every[1:], key=lambda o: (-(2 - abs(o[0] - 2)) - (2 - abs(o[1] - 2)), o))
+
+
+def row_offsets(nr):
+    return sorted(range(1, nr), key=lambda k: -min(k, nr - k))
 
 
 def col_peer(me, away, nc):
@@ -133,6 +137,15 @@
 ):
     mr = lax.axis_index("row")
     mc = lax.axis_index("col")
+    barrier = pltpu.get_barrier_semaphore()
+    for away in col_offsets(nc):
+        pl.semaphore_signal(
+            barrier, inc=1, device_id=(mr, col_peer(mc, away, nc)), device_id_type=MESH
+        )
+    for away in row_offsets(nr):
+        pl.semaphore_signal(
+            barrier, inc=1, device_id=(lax.rem(mr + away, nr), mc), device_id_type=MESH
+        )
     loads = [
         pltpu.make_async_copy(src, dst, load_sem.at[n])
         for n, (src, dst) in enumerate(
@@ -154,23 +167,6 @@
     ]
     for load in loads:
         load.start()
-    barrier = pltpu.get_barrier_semaphore()
-
-    def greet_col(k, carry):
-        pl.semaphore_signal(
-            barrier, inc=1, device_id=(mr, lax.rem(mc + k, nc)), device_id_type=MESH
-        )
-        return carry
-
-    def greet_row(k, carry):
-        pl.semaphore_signal(
-            barrier, inc=1, device_id=(lax.rem(mr + k, nr), mc), device_id_type=MESH
-        )
-        return carry
-
-    lax.fori_loop(1, nc, greet_col, 0)
-    lax.fori_loop(1, nr, greet_row, 0)
-
     moved_rows = COL_SENT * (nc - 1) + ROW_ROWS * (nr - 1)
     row_base = COL_ROWS * nc
 
@@ -310,7 +306,7 @@
                 device_id=(mr, peer),
                 device_id_type=MESH,
             ).start()
-        for away in sorted(range(1, nr), key=lambda k: -min(k, nr - k)):
+        for away in row_offsets(nr):
             peer = lax.rem(mr + away, nr)
             pltpu.make_async_remote_copy(
                 src_ref=sbuf.at[e, rows_at(row_base + ROW_ROWS * peer, ROW_ROWS)],

time: 33.5 us -> 33.2 us (level)
  no operation moved by 1% of the time
where the time goes in v4:
time: 33.2 us; the launch traced here: 33.1 us
  Pallas kernels  31.4 us (95%)
  other arithmetic  1.73 us (5%)
    pallas_call x1, Pallas kernels, on_device(): pl.pallas_call(functools.partial(kernel, nr, nc), out_shape=jax.ShapeDtyp...  31.4 us
    add x1, other arithmetic, on_device(): return 0.5 * cot_final + out.transpose(1, 0, 2)  1.73 us

profile of v4, /device:TPU:1, one launch (start us, length us, event | category | flops | bytes accessed | tf_op | source)
XLA Modules:
  0.0 33.1 jit_solution(16411024934032312082)
XLA Ops:
  0.0 0.0 copy-start
  0.0 31.4 %shard_map.118 = f32[5,125,128]{2,1,0:T(8,128)} custom-call(f32[5,125,128]{2,1,0:T(8,128)} %bitcast.6, f32[5,125,128]{2,1,0:T(8,128)} %bitcast.5, f32[1,128]{1,0:T(1,128)} %bitcast.7, s32[1,160]{1,0:T(1,128)} %col_hbm.1, s32[1,64]{1,0:T(1,128)} %row_hbm.1, s32[1,768]{1,0:T(1,128)} %ext_hbm.1, s32[1,768]{1,0:T(1,128)} %kind_hbm.1, s32[1,128]{1,0:T(1,128)} %fine_hbm.1, ...), custom_call_target="tpu_custom_call" | custom-call | tf_op jit(solution)/shard_map/pallas_call | solution.py:704
  31.4 0.0 copy-done
  31.4 1.7 %bitcast_add_fusion = f32[125,5,128]{2,0,1:T(8,128)} fusion(f32[5,125,128]{2,1,0:T(8,128)} %shard_map.118, f32[125,5,128]{2,0,1:T(8,128)S(1)} %copy-done), kind=kLoop, calls=%fused_computation | loop fusion | flops 160000 | bytes 960000 | tf_op jit(solution)/shard_map/add | solution.py:738
Async XLA Ops:
  0.0 31.4 %copy-start = (f32[125,5,128]{2,0,1:T(8,128)S(1)}, f32[125,5,128]{2,0,1:T(8,128)}, u32[]{:S(2)}) copy-start(f32[125,5,128]{2,0,1:T(8,128)} %param.13) | copy-start | bytes 960004
